TPU v7x, 32 devices: a whole 2x2x4 slice. The times are simulated.
32 devices in a mesh: fsdp: 16 (over z, x, core), tok: 2 (over y).
Axes of the slice: x: 2, y: 2, z: 4, core: 2. Of those that a mesh axis runs over, the one named last changes fastest.
Arguments:
- tokens: bfloat16 [2048, 2048], P('fsdp', 'tok'), may hold values from -6 to 6
- expert_ids: int32 [2048, 4], P('fsdp'), may hold values from 0 to 31, all different within a row; in each aligned block of 128 rows (0 to 127, 128 to 255, ...) at most 32 rows name the same one
- gate_probs: float32 [2048, 4], P('fsdp'), may hold values from 0.05 to 1
- w_gate: bfloat16 [32, 1408, 2048], P('fsdp', 'tok'), may hold values from -0.125 to 0.125
- w_up: bfloat16 [32, 1408, 2048], P('fsdp', 'tok'), may hold values from -0.125 to 0.125
- w_down: bfloat16 [32, 1408, 2048], P('fsdp', 'tok'), may hold values from -0.15625 to 0.15625
- grad_out: bfloat16 [2048, 2048], P('fsdp', 'tok'), may hold values from -6 to 6
Outputs:
- layer_out: bfloat16 [2048, 2048], P('fsdp', 'tok')
- d_tokens: bfloat16 [2048, 2048], P('fsdp', 'tok')
- d_gate_probs: float32 [2048, 4], P('fsdp')
- d_w_gate: float32 [32, 1408, 2048], P('fsdp', 'tok')
- d_w_up: float32 [32, 1408, 2048], P('fsdp', 'tok')
- d_w_down: float32 [32, 1408, 2048], P('fsdp', 'tok')
Inputs may be any that keep to these rules, and one draw needn't show every extreme that they name: `expert_ids`: each token names 4 different experts. Among the tokens of one index of fsdp (aligned blocks of 128 tokens) no expert is named more than 32 times, a bound that some block reaches.
All inputs are finite; a program needn't handle non-finite values.
Results may differ from a plain program's by a relative error of at most 0.0064.
Values may be sent and summed in bfloat16 or wider, within the bound.
A program may use at most 128 MiB of HBM per device.

v0:
```python
import jax
import jax.numpy as jnp
from jax import lax
from jax.sharding import PartitionSpec as P

TOPK = 4
EXPERTS = 32
CAP = 32


def route_slots(expert_ids):
    flat = expert_ids.reshape(-1)
    onehot = (flat[:, None] == jnp.arange(EXPERTS, dtype=jnp.int32)[None, :]).astype(jnp.int32)
    position = jnp.sum(jnp.cumsum(onehot, axis=0) * onehot, axis=1) - 1
    return flat * CAP + position


def fill_buffer(slot, values):
    width = values.shape[1]
    buffer = jnp.zeros((EXPERTS * CAP, width), jnp.bfloat16).at[slot].set(values)
    return buffer.reshape(EXPERTS, CAP, width)


def on_device(tokens, expert_ids, gate_probs, w_gate, w_up, w_down, grad_out):
    tok_rows, slice_width = tokens.shape
    slot = route_slots(expert_ids)
    owner = jnp.arange(tok_rows * TOPK, dtype=jnp.int32) // TOPK
    features = lax.all_gather(tokens, "tok", axis=1, tiled=True)
    received = lax.all_to_all(
        fill_buffer(slot, features[owner]), "fsdp", split_axis=0, concat_axis=1, tiled=True
    )
    gate = jnp.einsum("erd,ehd->erh", received, w_gate, preferred_element_type=jnp.float32)
    upper = jnp.einsum("erd,ehd->erh", received, w_up, preferred_element_type=jnp.float32)
    sigma = jax.nn.sigmoid(gate)
    active = gate * sigma
    hidden = (active * upper).astype(jnp.bfloat16)
    partial_out = jnp.einsum("erh,ehd->erd", hidden, w_down, preferred_element_type=jnp.float32)
    expert_out = lax.psum_scatter(partial_out, "tok", scatter_dimension=2, tiled=True).astype(
        jnp.bfloat16
    )
    returned = lax.all_to_all(expert_out, "fsdp", split_axis=1, concat_axis=0, tiled=True)
    route_out = (
        returned.reshape(EXPERTS * CAP, slice_width)[slot]
        .reshape(tok_rows, TOPK, slice_width)
        .astype(jnp.float32)
    )
    probs = gate_probs[:, :, None]
    layer_out = jnp.sum(probs * route_out, axis=1).astype(jnp.bfloat16)
    cotangent = grad_out.astype(jnp.float32)
    d_gate_probs = lax.psum(jnp.sum(cotangent[:, None, :] * route_out, axis=2), "tok")
    full_cotangent = lax.all_gather(grad_out, "tok", axis=1, tiled=True)
    scaled = (probs * full_cotangent[:, None, :].astype(jnp.float32)).astype(jnp.bfloat16)
    scaled = scaled.reshape(tok_rows * TOPK, full_cotangent.shape[1])
    d_expert_out = lax.all_to_all(
        fill_buffer(slot, scaled), "fsdp", split_axis=0, concat_axis=1, tiled=True
    )
    d_hidden = jnp.einsum("erd,ehd->erh", d_expert_out, w_down, preferred_element_type=jnp.float32)
    d_w_down = jnp.einsum("erh,erd->ehd", hidden, d_expert_out, preferred_element_type=jnp.float32)
    d_gate = (d_hidden * upper * sigma * (1.0 + gate * (1.0 - sigma))).astype(jnp.bfloat16)
    d_upper = (d_hidden * active).astype(jnp.bfloat16)
    d_w_gate = jnp.einsum("erh,erd->ehd", d_gate, received, preferred_element_type=jnp.float32)
    d_w_up = jnp.einsum("erh,erd->ehd", d_upper, received, preferred_element_type=jnp.float32)
    partial_in = jnp.einsum("erh,ehd->erd", d_gate, w_gate, preferred_element_type=jnp.float32)
    partial_in = partial_in + jnp.einsum(
        "erh,ehd->erd", d_upper, w_up, preferred_element_type=jnp.float32
    )
    d_rows = lax.psum_scatter(partial_in, "tok", scatter_dimension=2, tiled=True).astype(
        jnp.bfloat16
    )
    back_rows = lax.all_to_all(d_rows, "fsdp", split_axis=1, concat_axis=0, tiled=True)
    route_grad = back_rows.reshape(EXPERTS * CAP, slice_width)[slot].reshape(
        tok_rows, TOPK, slice_width
    )
    d_tokens = jnp.sum(route_grad.astype(jnp.float32), axis=1).astype(jnp.bfloat16)
    return (layer_out, d_tokens, d_gate_probs, d_w_gate, d_w_up, d_w_down)


def solution(mesh):
    return jax.shard_map(
        on_device,
        mesh=mesh,
        in_specs=(
            P("fsdp", "tok"),
            P("fsdp", None),
            P("fsdp", None),
            P("fsdp", "tok", None),
            P("fsdp", "tok", None),
            P("fsdp", "tok", None),
            P("fsdp", "tok"),
        ),
        out_specs=(
            P("fsdp", "tok"),
            P("fsdp", "tok"),
            P("fsdp", None),
            P("fsdp", "tok", None),
            P("fsdp", "tok", None),
            P("fsdp", "tok", None),
        ),
        check_vma=False,
    )
```

profile of v0, /device:TPU:11, one launch (start us, length us, event | category | flops | bytes accessed | tf_op | source)
XLA Modules:
  0.0 525.5 jit_solution(4761217609656714023)
XLA Ops:
  10.7 8.1 %all_gather.6 = bf16[128,2048]{1,0:T(8,128)(2,1)S(1)} all-gather(bf16[128,1024]{1,0:T(8,128)(2,1)} %param.7), channel_id=1, replica_groups=mesh['fsdp'=16,'tok'=2] {'tok'}, dimensions={1}, use_global_device_ids=true | all-gather | bytes 786432 | tf_op jit(solution)/shard_map/all_gather | solution.py:28
  18.7 13.3 %scatter_custom_fusion = bf16[1024,2048]{1,0:T(8,128)(2,1)} fusion(s32[512]{0:T(512)S(1)} %bitcast.71, bf16[128,2048]{1,0:T(8,128)(2,1)S(1)} %all_gather.6, s32[1024]{0:T(1024)S(1)} %pad_clamp_fusion.1, bf16[]{:T(256)} %constant.28.clone.1), kind=kCustom, calls=%fused_computation.13 | custom fusion | bytes 4194306 | tf_op jit(solution)/shard_map/scatter | solution.py:20
  32.1 7.6 %all-to-all-start = ((bf16[32,32,2048]{2,1,0:T(8,128)(2,1)}), bf16[32,32,2048]{2,1,0:T(8,128)(2,1)}, u32[]{:S(2)}, u32[]{:S(2)}) async-start(bf16[32,32,2048]{2,1,0:T(8,128)(2,1)} %bitcast.59), calls=%async_computation | async-start | bytes 8388608 | tf_op jit(solution)/shard_map/all_to_all | solution.py:29
  39.9 8.3 %all_gather.7 = bf16[128,2048]{1,0:T(8,128)(2,1)S(1)} all-gather(bf16[128,1024]{1,0:T(8,128)(2,1)S(1)} %copy-done.5), channel_id=1, replica_groups=mesh['fsdp'=16,'tok'=2] {'tok'}, dimensions={1}, use_global_device_ids=true | all-gather | bytes 786432 | tf_op jit(solution)/shard_map/all_gather | solution.py:51
  48.2 3.1 mul.88
  51.3 5.3 %mul.89 = f32[512,2048]{1,0:T(8,128)} reshape(f32[128,4,2048]{2,1,0:T(4,128)} %mul.88) | data formatting | bytes 8388608 | tf_op jit(solution)/shard_map/mul | solution.py:52
  56.6 8.0 %scatter_custom_fusion.1 = bf16[1024,2048]{1,0:T(8,128)(2,1)} fusion(s32[512]{0:T(512)S(1)} %bitcast.72, f32[512,2048]{1,0:T(8,128)} %mul.89, f32[512]{0:T(512)S(1)} %mul.86, bf16[]{:T(256)} %constant.28.clone.1), kind=kCustom, calls=%fused_computation.12 | custom fusion | flops 2097152 | bytes 8390658 | tf_op jit(solution)/shard_map/scatter | solution.py:20
  64.5 67.6 %all-to-all-done = bf16[32,32,2048]{2,1,0:T(8,128)(2,1)} async-done(((bf16[32,32,2048]{2,1,0:T(8,128)(2,1)}), bf16[32,32,2048]{2,1,0:T(8,128)(2,1)}, u32[]{:S(2)}, u32[]{:S(2)}) %all-to-all-start) | async-done | bytes 4194336 | tf_op jit(solution)/shard_map/all_to_all | solution.py:29
  132.1 5.0 all-to-all-start.2
  137.4 2.7 copy.31
  140.9 4.8 fusion.11
  145.6 4.8 fusion.10
  150.4 79.3 %all-to-all-done.2 = bf16[32,32,2048]{2,1,0:T(8,128)(2,1)} async-done(((bf16[32,32,2048]{2,1,0:T(8,128)(2,1)}), bf16[32,32,2048]{2,1,0:T(8,128)(2,1)}, u32[]{:S(2)}, u32[]{:S(2)}) %all-to-all-start.2) | async-done | bytes 4194336 | tf_op jit(solution)/shard_map/all_to_all | solution.py:54
  229.7 2.7 copy.35
  232.7 10.4 %multiply_convert_fusion.1 = (bf16[2,512,704]{1,2,0:T(8,128)(2,1)S(1)}, bf16[2,512,704]{1,2,0:T(8,128)(2,1)}, bf16[2,512,704]{1,2,0:T(8,128)(2,1)S(1)}) fusion(f32[2,512,704]{1,2,0:T(8,128)} %fusion.10, f32[2,512,704]{1,2,0:T(8,128)S(1)} %copy-done.11, bf16[2,512,2048]{2,1,0:T(8,128)(2,1)S(1)} %bitcast.69, bf16[2,704,2048]{2,1,0:T(8,128)(2,1)} %param.12), kind=kOutput, calls=%fused_computation.7 | convolution fusion | flops 2963603456 | bytes 20054016 | tf_op jit(solution)/shard_map/erd,ehd->erh/dot_general | solution.py:57
  244.2 5.8 %fusion.12 = f32[2,512,2048]{2,1,0:T(8,128)} fusion(bf16[2,512,704]{1,2,0:T(8,128)(2,1)S(1)} %get-tuple-element.16, bf16[2,704,2048]{2,1,0:T(8,128)(2,1)S(1)} %bitcast.77), kind=kOutput, calls=%fused_computation.40 | convolution fusion | flops 2952790016 | bytes 15597568 | tf_op jit(solution)/shard_map/erh,ehd->erd/dot_general | solution.py:37
  250.4 6.1 %fusion.13 = f32[2,512,2048]{2,1,0:T(8,128)S(1)} fusion(bf16[2,512,704]{1,2,0:T(8,128)(2,1)} %get-tuple-element.15, bf16[2,704,2048]{2,1,0:T(8,128)(2,1)} %param.10), kind=kOutput, calls=%fused_computation.41 | convolution fusion | flops 2952790016 | bytes 15597568 | tf_op jit(solution)/shard_map/erh,ehd->erd/dot_general | solution.py:63
  256.5 5.7 %convolution_add_fusion = f32[2,512,2048]{2,1,0:T(8,128)} fusion(f32[2,512,2048]{2,1,0:T(8,128)S(1)} %fusion.13, bf16[2,512,704]{1,2,0:T(8,128)(2,1)S(1)} %get-tuple-element.14, bf16[2,704,2048]{2,1,0:T(8,128)(2,1)S(1)} %bitcast.64), kind=kOutput, calls=%fused_computation.6 | convolution fusion | flops 2954887168 | bytes 23986176 | tf_op jit(solution)/shard_map/erh,ehd->erd/dot_general | solution.py:64
  262.3 86.7 %reduce-scatter.3.cloned.1.call-done = f32[2,512,1024]{2,1,0:T(8,128)} async-done(((f32[2,512,2048]{2,1,0:T(8,128)}), f32[2,512,1024]{2,1,0:T(8,128)}) %reduce-scatter.3.cloned.1.call-update) | async-done | bytes 4194320 | tf_op jit(solution)/shard_map/reduce_scatter | solution.py:38
  349.0 2.5 convert_element_type.48
  351.5 3.5 copy.32
  355.0 6.4 %all-to-all-start.1 = ((bf16[2,512,1024]{2,0,1:T(2,128)(2,1)}), bf16[2,512,1024]{2,0,1:T(2,128)(2,1)S(1)}, u32[]{:S(2)}, u32[]{:S(2)}) async-start(bf16[2,512,1024]{2,0,1:T(2,128)(2,1)} %copy.32), calls=%async_computation.2 | async-start | bytes 4194304 | tf_op jit(solution)/shard_map/all_to_all | solution.py:41
  361.4 89.9 %reduce-scatter.5.cloned.1.call-done = f32[2,512,1024]{2,1,0:T(8,128)} async-done(((f32[2,512,2048]{2,1,0:T(8,128)}), f32[2,512,1024]{2,1,0:T(8,128)}) %reduce-scatter.5.cloned.1.call-update) | async-done | bytes 4194320 | tf_op jit(solution)/shard_map/reduce_scatter | solution.py:67
  451.3 2.5 convert_element_type.56
  453.8 3.5 copy.36
  457.3 6.8 %all-to-all-start.3 = ((bf16[2,512,1024]{2,0,1:T(2,128)(2,1)}), bf16[2,512,1024]{2,0,1:T(2,128)(2,1)}, u32[]{:S(2)}, u32[]{:S(2)}) async-start(bf16[2,512,1024]{2,0,1:T(2,128)(2,1)} %copy.36), calls=%async_computation.5 | async-start | bytes 4194304 | tf_op jit(solution)/shard_map/all_to_all | solution.py:70
  465.9 10.4 %fusion.16 = f32[2,704,2048]{2,1,0:T(8,128)} fusion(bf16[2,512,704]{1,2,0:T(8,128)(2,1)} %copy-done.10, bf16[2,512,2048]{2,1,0:T(8,128)(2,1)} %bitcast.70), kind=kOutput, calls=%fused_computation.44 | convolution fusion | flops 2952790016 | bytes 17170432 | tf_op jit(solution)/shard_map/erh,erd->ehd/dot_general | solution.py:58
  476.2 6.2 %fusion.15 = f32[2,704,2048]{2,1,0:T(8,128)} fusion(bf16[2,512,704]{1,2,0:T(8,128)(2,1)S(1)} %get-tuple-element.14, bf16[2,512,2048]{2,1,0:T(8,128)(2,1)S(1)} %bitcast.67), kind=kOutput, calls=%fused_computation.43 | convolution fusion | flops 2952790016 | bytes 17170432 | tf_op jit(solution)/shard_map/erh,erd->ehd/dot_general | solution.py:62
  482.4 6.1 %fusion.14 = f32[2,704,2048]{2,1,0:T(8,128)} fusion(bf16[2,512,704]{1,2,0:T(8,128)(2,1)S(1)} %copy-done.9, bf16[2,512,2048]{2,1,0:T(8,128)(2,1)S(1)} %bitcast.68), kind=kOutput, calls=%fused_computation.42 | convolution fusion | flops 2952790016 | bytes 17170432 | tf_op jit(solution)/shard_map/erh,erd->ehd/dot_general | solution.py:61
  492.0 3.6 multiply_reduce_fusion
  495.6 6.2 %psum.7 = f32[128,4]{1,0:T(8,128)S(1)} all-reduce(f32[128,4]{1,0:T(8,128)S(1)} %get-tuple-element.12), channel_id=1, replica_groups=mesh['fsdp'=16,'tok'=2] {'tok'}, use_global_device_ids=true, to_apply=%region_10.11 | all-reduce | flops 512 | bytes 4096 | tf_op jit(solution)/shard_map/psum | solution.py:50
  502.5 8.9 %all-to-all-done.3 = bf16[2,512,1024]{2,0,1:T(2,128)(2,1)} async-done(((bf16[2,512,1024]{2,0,1:T(2,128)(2,1)}), bf16[2,512,1024]{2,0,1:T(2,128)(2,1)}, u32[]{:S(2)}, u32[]{:S(2)}) %all-to-all-start.3) | async-done | bytes 2097184 | tf_op jit(solution)/shard_map/all_to_all | solution.py:70
  (77 shorter events, 19.2 us)
Async XLA Ops:
  32.1 7.6 %copy-start.8 = (f32[128,4]{0,1:T(4,128)S(1)}, f32[128,4]{0,1:T(4,128)}, u32[]{:S(2)}) copy-start(f32[128,4]{0,1:T(4,128)} %param.9) | copy-start | bytes 6148
  32.1 7.8 %copy-start.5 = (bf16[128,1024]{1,0:T(8,128)(2,1)S(1)}, bf16[128,1024]{1,0:T(8,128)(2,1)}, u32[]{:S(2)}) copy-start(bf16[128,1024]{1,0:T(8,128)(2,1)} %param.13) | copy-start | bytes 786436
  32.1 100.0 %all-to-all-start = ((bf16[32,32,2048]{2,1,0:T(8,128)(2,1)}), bf16[32,32,2048]{2,1,0:T(8,128)(2,1)}, u32[]{:S(2)}, u32[]{:S(2)}) async-start(bf16[32,32,2048]{2,1,0:T(8,128)(2,1)} %bitcast.59), calls=%async_computation | async-start | bytes 8388608 | tf_op jit(solution)/shard_map/all_to_all | solution.py:29
  39.8 16.8 %copy-start.6 = (f32[128,4]{1,0:T(8,128)}, f32[128,4]{1,0:T(8,128)S(1)}, u32[]{:S(2)}) copy-start(f32[128,4]{1,0:T(8,128)S(1)} %copy.26) | copy-start | bytes 6148
  132.1 8.0 %slice-start = ((s8[5767168]{0:T(1024)(128)(4,1)}), s8[1572864]{0:T(1024)(128)(4,1)S(1)}, s32[]{:S(2)}) async-start(s8[5767168]{0:T(1024)(128)(4,1)} %bitcast.61), calls=%async_computation.8 | async-start | bytes 3145728
  132.1 97.5 %all-to-all-start.2 = ((bf16[32,32,2048]{2,1,0:T(8,128)(2,1)}), bf16[32,32,2048]{2,1,0:T(8,128)(2,1)}, u32[]{:S(2)}, u32[]{:S(2)}) async-start(bf16[32,32,2048]{2,1,0:T(8,128)(2,1)} %bitcast.58), calls=%async_computation.3 | async-start | bytes 8388608 | tf_op jit(solution)/shard_map/all_to_all | solution.py:54
  137.2 211.8 %reduce-scatter.3.cloned.1.call-start = ((), (), s32[]{:S(2)}) async-start(), calls=%async_computation.6 | async-start | bytes 12582912 | tf_op jit(solution)/shard_map/reduce_scatter | solution.py:38
  137.4 3.5 slice-start.1
  137.4 8.2 %slice-start.6 = ((s8[5767168]{0:T(1024)(128)(4,1)}), s8[4194304]{0:T(1024)(128)(4,1)S(1)}, s32[]{:S(2)}) async-start(s8[5767168]{0:T(1024)(128)(4,1)} %bitcast.78), calls=%async_computation.14 | async-start | bytes 8388608
  140.1 5.5 %copy-start.2 = (bf16[2,16,32,2048]{3,2,1,0:T(8,128)(2,1)}, bf16[2,16,32,2048]{3,2,1,0:T(8,128)(2,1)S(1)}, u32[]{:S(2)}) copy-start(bf16[2,16,32,2048]{3,2,1,0:T(8,128)(2,1)S(1)} %copy.31) | copy-start | bytes 12582916
  140.9 4.8 slice-start.7
  229.7 3.1 copy-start.11
  229.7 14.6 %slice-start.4 = ((s8[5767168]{0:T(1024)(128)(4,1)}), s8[4194304]{0:T(1024)(128)(4,1)S(1)}, s32[]{:S(2)}) async-start(s8[5767168]{0:T(1024)(128)(4,1)} %bitcast.76), calls=%async_computation.12 | async-start | bytes 8388608
  232.3 10.8 %copy-start.4 = (bf16[2,16,32,2048]{3,2,1,0:T(8,128)(2,1)}, bf16[2,16,32,2048]{3,2,1,0:T(8,128)(2,1)S(1)}, u32[]{:S(2)}) copy-start(bf16[2,16,32,2048]{3,2,1,0:T(8,128)(2,1)S(1)} %copy.35) | copy-start | bytes 12582916
  232.7 11.5 %slice-start.5 = ((s8[5767168]{0:T(1024)(128)(4,1)}), s8[1572864]{0:T(1024)(128)(4,1)S(1)}, s32[]{:S(2)}) async-start(s8[5767168]{0:T(1024)(128)(4,1)} %bitcast.76), calls=%async_computation.13 | async-start | bytes 3145728
  243.1 1.1 copy-start.10
  250.1 6.4 %slice-start.2 = ((s8[5767168]{0:T(1024)(128)(4,1)}), s8[1572864]{0:T(1024)(128)(4,1)S(1)}, s32[]{:S(2)}) async-start(s8[5767168]{0:T(1024)(128)(4,1)} %bitcast.63), calls=%async_computation.10 | async-start | bytes 3145728
  250.1 201.2 %reduce-scatter.5.cloned.1.call-start = ((), (), s32[]{:S(2)}) async-start(), calls=%async_computation.7 | async-start | bytes 12582912 | tf_op jit(solution)/shard_map/reduce_scatter | solution.py:67
  250.4 6.1 %slice-start.3 = ((s8[5767168]{0:T(1024)(128)(4,1)}), s8[4194304]{0:T(1024)(128)(4,1)S(1)}, s32[]{:S(2)}) async-start(s8[5767168]{0:T(1024)(128)(4,1)} %bitcast.63), calls=%async_computation.11 | async-start | bytes 8388608
  355.0 102.3 %all-to-all-start.1 = ((bf16[2,512,1024]{2,0,1:T(2,128)(2,1)}), bf16[2,512,1024]{2,0,1:T(2,128)(2,1)S(1)}, u32[]{:S(2)}, u32[]{:S(2)}) async-start(bf16[2,512,1024]{2,0,1:T(2,128)(2,1)} %copy.32), calls=%async_computation.2 | async-start | bytes 4194304 | tf_op jit(solution)/shard_map/all_to_all | solution.py:41
  457.3 19.0 %copy-start = (bf16[2,512,1024]{2,0,1:T(2,128)(2,1)}, bf16[2,512,1024]{2,0,1:T(2,128)(2,1)S(1)}, u32[]{:S(2)}) copy-start(bf16[2,512,1024]{2,0,1:T(2,128)(2,1)S(1)} %all-to-all-done.1) | copy-start | bytes 6291460
  457.3 54.1 %all-to-all-start.3 = ((bf16[2,512,1024]{2,0,1:T(2,128)(2,1)}), bf16[2,512,1024]{2,0,1:T(2,128)(2,1)}, u32[]{:S(2)}, u32[]{:S(2)}) async-start(bf16[2,512,1024]{2,0,1:T(2,128)(2,1)} %copy.36), calls=%async_computation.5 | async-start | bytes 4194304 | tf_op jit(solution)/shard_map/all_to_all | solution.py:70
  465.9 10.4 %copy-start.3 = (bf16[2,16,32,2048]{3,2,1,0:T(8,128)(2,1)S(1)}, bf16[2,16,32,2048]{3,2,1,0:T(8,128)(2,1)}, u32[]{:S(2)}) copy-start(bf16[2,16,32,2048]{3,2,1,0:T(8,128)(2,1)} %copy-done.2) | copy-start | bytes 12582916
  476.2 6.2 %copy-start.9 = (bf16[2,512,704]{1,2,0:T(8,128)(2,1)S(1)}, bf16[2,512,704]{1,2,0:T(8,128)(2,1)}, u32[]{:S(2)}) copy-start(bf16[2,512,704]{1,2,0:T(8,128)(2,1)} %get-tuple-element.15) | copy-start | bytes 4325380
  482.4 6.1 %copy-start.1 = (bf16[2,512,1024]{2,0,1:T(2,128)(2,1)S(1)}, bf16[2,512,1024]{2,0,1:T(2,128)(2,1)}, u32[]{:S(2)}) copy-start(bf16[2,512,1024]{2,0,1:T(2,128)(2,1)} %copy-done) | copy-start | bytes 6291460
  489.2 2.8 copy-start.7
Sparse Core Ops, SparseCore 0:
  250.2 98.7 reduce-scatter.2
  352.0 99.2 reduce-scatter.4
where the time goes:
time: 534 us; the launch traced here: 526 us
  waiting for transfers between devices  332 us (62%)
  matrix products  60.2 us (11%)
  local copies, waits for them, and re-layouts  46.7 us (9%)
  starting transfers between devices  26.2 us (5%)
  blocking collectives  22.6 us (4%)
  other arithmetic  22.5 us (4%)
  between operations  14.8 us (3%)
    reduce_scatter x1, waiting for transfers between devices, on_device(): lax.psum_scatter(partial_in, 'tok', scatter_dimension=2, tiled=True)  89.9 us
    reduce_scatter x1, waiting for transfers between devices, on_device(): lax.psum_scatter(partial_out, 'tok', scatter_dimension=2, tiled=True)  86.7 us
    all_to_all x1, waiting for transfers between devices, on_device(): lax.all_to_all(fill_buffer(slot, scaled), 'fsdp', split_axis=0, concat_ax...  79.3 us
    all_to_all x1, waiting for transfers between devices, on_device(): lax.all_to_all(fill_buffer(slot, features[owner]), 'fsdp', split_axis=0,...  67.6 us
    scatter x1, local copies, waits for them, and re-layouts, fill_buffer(): jnp.zeros((EXPERTS * CAP, width), jnp.bfloat16).at[slot].set(values)  13.3 us
  transfers between devices with their start and end apart: 6, of which 5 were waited for; matrix products, arithmetic and copies ran while one was open for 16% of the time, Pallas kernels for 0%

commit v1 on v0

v1 whole, which is shorter than its diff:
```python
import functools

import jax
import jax.numpy as jnp
from jax import lax
from jax.experimental import pallas as pl
from jax.experimental.pallas import tpu as pltpu
from jax.sharding import PartitionSpec as P

CAP = 32
MESH = pl.DeviceIdType.MESH


def flip(bit, change):
    return 1 - bit if change else bit


class Place:
    def __init__(self):
        f = lax.axis_index("fsdp")
        self.t = lax.axis_index("tok")
        self.core = f % 2
        self.x = (f // 2) % 2
        self.z0 = (f // 4) % 2
        self.z1 = f // 8

    def block(self, dz=0, dx=0, dc=0):
        z = flip(self.z1, dz // 2) * 2 + flip(self.z0, dz % 2)
        return z * 4 + flip(self.x, dx) * 2 + flip(self.core, dc)

    def device(self, dz=0, dx=0, dy=0, dc=0):
        return (self.block(dz, dx, dc), flip(self.t, dy))

    def columns(self, dy, width):
        return pl.ds(pl.multiple_of(flip(self.t, dy) * width, width), width)

    def partners(self):
        return [self.device(dz=d) for d in (1, 2, 3)] + [
            self.device(dx=1),
            self.device(dy=1),
            self.device(dc=1),
        ]


def greet(place):
    barrier = pltpu.get_barrier_semaphore()
    partners = place.partners()
    for partner in partners:
        pl.semaphore_signal(barrier, inc=1, device_id=partner, device_id_type=MESH)
    pl.semaphore_wait(barrier, len(partners))


def gather_kernel(in0, in1, out0, out1, send_sem, recv_sem, core_sem, own_sem):
    place = Place()
    ins, outs = (in0, in1), (out0, out1)
    rows, width = in0.shape
    half = rows // 2
    sent = []

    def where(a, h, dz, dx, dy, dc=0):
        return outs[a].at[
            place.block(dz, dx, dc), pl.ds(h * half, half), place.columns(dy, width)
        ]

    def send(a, h, dz, dx, dy, to, sem):
        own = dz == dx == dy == 0
        source = ins[a].at[pl.ds(h * half, half)] if own else where(a, h, dz, dx, dy)
        copy = pltpu.make_async_remote_copy(
            src_ref=source,
            dst_ref=where(a, h, dz, dx, dy),
            send_sem=send_sem.at[len(sent)],
            recv_sem=sem,
            device_id=to,
            device_id_type=MESH,
        )
        copy.start()
        sent.append(copy)

    def index(a, h, dz, dx, dy):
        return (((a * 2 + h) * 4 + dz) * 2 + dx) * 2 + dy

    def wait(a, h, dz, dx, dy, dc=0):
        place_here = where(a, h, dz, dx, dy, dc)
        sem = (core_sem if dc else recv_sem).at[index(a, h, dz, dx, dy)]
        pltpu.make_async_copy(place_here, place_here, sem).wait()

    def to_core(a, h, dz, dx, dy):
        send(a, h, dz, dx, dy, place.device(dc=1), core_sem.at[index(a, h, dz, dx, dy)])

    def to_x(a, h, dz, dy):
        send(a, h, dz, 0, dy, place.device(dx=1), recv_sem.at[index(a, h, dz, 1, dy)])

    def to_y(a, h, dz, dx):
        send(a, h, dz, dx, 0, place.device(dy=1), recv_sem.at[index(a, h, dz, dx, 1)])

    own_copies = [
        pltpu.make_async_copy(
            ins[a], outs[a].at[place.block(), :, place.columns(0, width)], own_sem.at[a]
        )
        for a in range(2)
    ]
    for copy in own_copies:
        copy.start()
    greet(place)
    events = []
    for a in range(2):
        for h in range(2):
            for dz in range(1, 4):
                events.append((a * 3, "z", a, h, dz))
            for dz in range(4):
                events.append((a * 30 + dz * 5 + 1, "column", a, h, dz))
                events.append((a * 30 + dz * 5 + 12, "plane", a, h, dz))
                events.append((a * 30 + dz * 5 + 22, "last", a, h, dz))
    for _, kind, a, h, dz in sorted(events):
        if kind == "z":
            send(a, h, 0, 0, 0, place.device(dz=dz), recv_sem.at[index(a, h, dz, 0, 0)])
        elif kind == "column":
            if dz:
                wait(a, h, dz, 0, 0)
            if h == 0:
                to_x(a, h, dz, 0)
                to_y(a, h, dz, 0)
            else:
                to_y(a, h, dz, 0)
                to_x(a, h, dz, 0)
            to_core(a, h, dz, 0, 0)
        elif kind == "plane":
            if h == 0:
                wait(a, h, dz, 1, 0)
                to_y(a, h, dz, 1)
                to_core(a, h, dz, 1, 0)
            else:
                wait(a, h, dz, 0, 1)
                to_x(a, h, dz, 1)
                to_core(a, h, dz, 0, 1)
        else:
            dx, dy = (0, 1) if h == 0 else (1, 0)
            wait(a, h, dz, dx, dy)
            to_core(a, h, dz, dx, dy)
            wait(a, h, dz, 1, 1)
            to_core(a, h, dz, 1, 1)
    for a in range(2):
        for h in range(2):
            for dz in range(4):
                for dx in range(2):
                    for dy in range(2):
                        wait(a, h, dz, dx, dy, 1)
    for copy in sent:
        copy.wait_send()
    for copy in own_copies:
        copy.wait()


def gather_pair(first, second):
    rows, width = first.shape
    full = jax.ShapeDtypeStruct((16, rows, 2 * width), first.dtype)
    return pl.pallas_call(
        gather_kernel,
        out_shape=(full, full),
        in_specs=[pl.BlockSpec(memory_space=pl.ANY)] * 2,
        out_specs=[pl.BlockSpec(memory_space=pl.ANY)] * 2,
        scratch_shapes=[
            pltpu.SemaphoreType.DMA((124,)),
            pltpu.SemaphoreType.DMA((64,)),
            pltpu.SemaphoreType.DMA((64,)),
            pltpu.SemaphoreType.DMA((2,)),
        ],
        compiler_params=pltpu.CompilerParams(collective_id=0, has_side_effects=True),
    )(first, second)


def scatter_kernel(
    in0, in1, out0, out1, core_buf, wide_buf, near_buf, z_buf, send_sem, core_sem, wide_sem, near_sem, z_sem
):
    place = Place()
    ins, outs = (in0, in1), (out0, out1)
    half, width = core_buf.shape[-2:]
    sent = []

    def send(source, target, sem, to):
        copy = pltpu.make_async_remote_copy(
            src_ref=source,
            dst_ref=target,
            send_sem=send_sem.at[len(sent)],
            recv_sem=sem,
            device_id=to,
            device_id_type=MESH,
        )
        copy.start()
        sent.append(copy)

    def arrive(buffer, sem):
        pltpu.make_async_copy(buffer, buffer, sem).wait()

    def add(target, source):
        def step(i, carry):
            at = pl.ds(pl.multiple_of(i * 16, 16), 16)
            target[at, :] = target[at, :] + source[at, :]
            return carry

        lax.fori_loop(0, half // 16, step, 0)

    def part(a, h, dz, dx, dy, dc):
        return ins[a].at[
            place.block(dz, dx, dc), pl.ds(h * half, half), place.columns(dy, width)
        ]

    def slot(a, h, dz, dx, dy):
        return (((a * 2 + h) * 4 + dz) * 2 + dx) * 2 + dy

    greet(place)
    order = [3, 2, 1, 0]
    events = []
    for a in range(2):
        for n, dz in enumerate(order):
            for h in range(2):
                events.append((a * 30 + n * 2 - 40, "core", a, h, dz))
                events.append((a * 30 + n * 6 + 4, "wide", a, h, dz))
                events.append((a * 30 + n * 6 + 14, "near", a, h, dz))
                events.append((a * 30 + n * 6 + 22, "z", a, h, dz))
    for _, kind, a, h, dz in sorted(events):
        pair = (a * 2 + h) * 4 + dz
        across = place.device(dy=1) if h == 0 else place.device(dx=1)
        along = place.device(dx=1) if h == 0 else place.device(dy=1)
        if kind == "core":
            for far in (1, 0):
                for other in (1, 0):
                    dx, dy = (other, far) if h == 0 else (far, other)
                    k = slot(a, h, dz, dx, dy)
                    send(part(a, h, dz, dx, dy, 1), core_buf.at[k], core_sem.at[k], place.device(dc=1))
        elif kind == "wide":
            for far in (1, 0):
                for other in (1, 0):
                    dx, dy = (other, far) if h == 0 else (far, other)
                    k = slot(a, h, dz, dx, dy)
                    arrive(core_buf.at[k], core_sem.at[k])
                    add(core_buf.at[k], part(a, h, dz, dx, dy, 0))
                    if far:
                        w = pair * 2 + other
                        send(core_buf.at[k], wide_buf.at[w], wide_sem.at[w], across)
        elif kind == "near":
            for other in (1, 0):
                dx, dy = (other, 0) if h == 0 else (0, other)
                w = pair * 2 + other
                arrive(wide_buf.at[w], wide_sem.at[w])
                add(wide_buf.at[w], core_buf.at[slot(a, h, dz, dx, dy)])
                if other:
                    send(wide_buf.at[w], near_buf.at[pair], near_sem.at[pair], along)
        else:
            arrive(near_buf.at[pair], near_sem.at[pair])
            add(near_buf.at[pair], wide_buf.at[pair * 2])
            if dz:
                send(near_buf.at[pair], z_buf.at[pair], z_sem.at[pair], place.device(dz=dz))
    for a in range(2):
        for h in range(2):
            pair = (a * 2 + h) * 4
            for dz in (3, 2, 1):
                arrive(z_buf.at[pair + dz], z_sem.at[pair + dz])

            def step(i, carry, a=a, h=h, pair=pair):
                at = pl.ds(pl.multiple_of(i * 16, 16), 16)
                total = near_buf[pair, at, :].astype(jnp.float32)
                for dz in (1, 2, 3):
                    total = total + z_buf[pair + dz, at, :].astype(jnp.float32)
                to = pl.ds(pl.multiple_of(h * half + i * 16, 16), 16)
                outs[a][to, :] = total.astype(outs[a].dtype)
                return carry

            lax.fori_loop(0, half // 16, step, 0)
    for copy in sent:
        copy.wait_send()


def scatter_pair(first, second):
    blocks, rows, full = first.shape
    half, width = rows // 2, full // 2
    out = jax.ShapeDtypeStruct((rows, width), first.dtype)
    return pl.pallas_call(
        scatter_kernel,
        out_shape=(out, out),
        in_specs=[pl.BlockSpec(memory_space=pltpu.VMEM)] * 2,
        out_specs=[pl.BlockSpec(memory_space=pltpu.VMEM)] * 2,
        scratch_shapes=[
            pltpu.VMEM((64, half, width), first.dtype),
            pltpu.VMEM((32, half, width), first.dtype),
            pltpu.VMEM((16, half, width), first.dtype),
            pltpu.VMEM((16, half, width), first.dtype),
            pltpu.SemaphoreType.DMA((124,)),
            pltpu.SemaphoreType.DMA((64,)),
            pltpu.SemaphoreType.DMA((32,)),
            pltpu.SemaphoreType.DMA((16,)),
            pltpu.SemaphoreType.DMA((16,)),
        ],
        compiler_params=pltpu.CompilerParams(
            collective_id=1, has_side_effects=True, vmem_limit_bytes=48 * 2**20
        ),
    )(first, second)


def gather_any(value):
    wide = lax.all_gather(value, "tok", axis=1, tiled=True)
    return lax.all_gather(wide, "fsdp", axis=0, tiled=False)


def scatter_any(value):
    blocks, rows, full = value.shape
    mine = lax.psum_scatter(
        value.reshape(blocks * rows, full), "fsdp", scatter_dimension=0, tiled=True
    )
    return lax.psum_scatter(mine, "tok", scatter_dimension=1, tiled=True)


def on_device(by_kernel, tokens, expert_ids, gate_probs, w_gate, w_up, w_down, grad_out):
    tok_rows, topk = expert_ids.shape
    local = w_gate.shape[0]
    f32 = jnp.float32
    me = lax.axis_index("fsdp")

    routes = jnp.concatenate([expert_ids.astype(f32).T, gate_probs.T], axis=0)
    routes = lax.all_gather(routes, "fsdp", axis=0, tiled=False)
    if by_kernel:
        all_tokens, all_grads = gather_pair(tokens, grad_out)
    else:
        all_tokens, all_grads = gather_any(tokens), gather_any(grad_out)
    blocks = all_tokens.shape[0]

    names = routes[:, :topk]
    mine = (me * local + jnp.arange(local, dtype=jnp.int32)).astype(f32)
    chosen = names[None] == mine[:, None, None, None]
    hit = jnp.any(chosen, axis=2)
    prob = jnp.sum(jnp.where(chosen, routes[None, :, topk:], 0.0), axis=2)
    before = jnp.triu(jnp.ones((tok_rows, tok_rows), jnp.bfloat16), 1)
    place = jnp.einsum("ebs,st->ebt", hit.astype(jnp.bfloat16), before, preferred_element_type=f32)
    place = jnp.where(hit, place, -1.0)
    filled = place[:, :, None, :] == jnp.arange(CAP, dtype=jnp.int32).astype(f32)[None, None, :, None]
    select = filled.astype(jnp.bfloat16)
    row_prob = jnp.sum(jnp.where(filled, prob[:, :, None, :], 0.0), axis=3)
    row_prob = row_prob.reshape(local, blocks * CAP, 1)

    def pick(values):
        rows = jnp.einsum("ebrt,btd->ebrd", select, values, preferred_element_type=f32)
        return rows.astype(jnp.bfloat16).reshape(local, blocks * CAP, values.shape[-1])

    def place_back(rows):
        rows = rows.astype(jnp.bfloat16).reshape(local, blocks, CAP, rows.shape[-1])
        values = jnp.einsum("ebrt,ebrd->btd", select, rows, preferred_element_type=f32)
        return values.astype(jnp.bfloat16)

    inputs = pick(all_tokens)
    cotangent = pick(all_grads)
    gate = jnp.einsum("erd,ehd->erh", inputs, w_gate, preferred_element_type=f32)
    upper = jnp.einsum("erd,ehd->erh", inputs, w_up, preferred_element_type=f32)
    raw = jnp.einsum("erd,ehd->erh", cotangent, w_down, preferred_element_type=f32)
    sigma = jax.nn.sigmoid(gate)
    active = gate * sigma
    hidden = active * upper
    weighted = (row_prob * hidden).astype(jnp.bfloat16)
    d_hidden = row_prob * raw
    d_gate = (d_hidden * upper * sigma * (1.0 + gate * (1.0 - sigma))).astype(jnp.bfloat16)
    d_upper = (d_hidden * active).astype(jnp.bfloat16)
    d_rows = jnp.sum(hidden * raw, axis=2).reshape(local, blocks, CAP)

    out_rows = jnp.einsum("erh,ehd->erd", weighted, w_down, preferred_element_type=f32)
    in_rows = jnp.einsum("erh,ehd->erd", d_gate, w_gate, preferred_element_type=f32)
    in_rows = in_rows + jnp.einsum("erh,ehd->erd", d_upper, w_up, preferred_element_type=f32)
    part_out, part_in = place_back(out_rows), place_back(in_rows)
    if by_kernel:
        layer_out, d_tokens = scatter_pair(part_out, part_in)
    else:
        layer_out, d_tokens = scatter_any(part_out), scatter_any(part_in)

    d_w_down = jnp.einsum("erh,erd->ehd", weighted, cotangent, preferred_element_type=f32)
    d_w_gate = jnp.einsum("erh,erd->ehd", d_gate, inputs, preferred_element_type=f32)
    d_w_up = jnp.einsum("erh,erd->ehd", d_upper, inputs, preferred_element_type=f32)

    d_prob = jnp.sum(jnp.where(filled, d_rows[:, :, :, None], 0.0), axis=2)
    d_prob = jnp.sum(jnp.where(chosen, d_prob[:, :, None, :], 0.0), axis=0)
    d_prob = lax.psum(d_prob.reshape(blocks, topk * tok_rows), ("fsdp", "tok"))
    d_prob = lax.dynamic_index_in_dim(d_prob, me, 0, keepdims=False)
    d_gate_probs = d_prob.reshape(topk, tok_rows).T
    return (layer_out, d_tokens, d_gate_probs, d_w_gate, d_w_up, d_w_down)


def solution(mesh):
    by_kernel = mesh.shape["fsdp"] == 16 and mesh.shape["tok"] == 2
    return jax.shard_map(
        functools.partial(on_device, by_kernel),
        mesh=mesh,
        in_specs=(
            P("fsdp", "tok"),
            P("fsdp", None),
            P("fsdp", None),
            P("fsdp", "tok", None),
            P("fsdp", "tok", None),
            P("fsdp", "tok", None),
            P("fsdp", "tok"),
        ),
        out_specs=(
            P("fsdp", "tok"),
            P("fsdp", "tok"),
            P("fsdp", None),
            P("fsdp", "tok", None),
            P("fsdp", "tok", None),
            P("fsdp", "tok", None),
        ),
        check_vma=False,
    )
```

time: 534 us -> 330 us (0.62)
  waiting for transfers between devices: 332 us -> 0 us
  Pallas kernels: 0 us -> 179 us
  local copies, waits for them, and re-layouts: 46.7 us -> 5.67 us
  blocking collectives: 22.6 us -> 54.8 us
  starting transfers between devices: 26.2 us -> 0 us
  matrix products: 60.2 us -> 79.5 us
  other arithmetic: 22.5 us -> 5.68 us
  between operations: 14.8 us -> 0.91 us
    pallas_call x0 -> x2, Pallas kernels: none -> 179 us  [the longest x1 89.5 us: gather_pair(): pl.pallas_call(gather_kernel, out_shape=(full, full), in_specs=[pl.BlockS...]
    reduce_scatter x2 -> x0, waiting for transfers between devices: 177 us -> none  [the longest x1 89.9 us: on_device(): lax.psum_scatter(partial_in, 'tok', scatter_dimension=2, tiled=True)]
    all_to_all x4 -> x0, waiting for transfers between devices: 156 us -> none  [the longest x1 79.3 us: on_device(): lax.all_to_all(fill_buffer(slot, scaled), 'fsdp', split_axis=0, concat_ax...]
    psum x1, blocking collectives: 6.24 us -> 39 us  [on_device(): d_prob = lax.psum(d_prob.reshape(blocks, topk * tok_rows), ('fsdp', 'tok'))]
    all_to_all x4 -> x0, starting transfers between devices: 25.8 us -> none  [the longest x1 7.57 us: on_device(): lax.all_to_all(fill_buffer(slot, features[owner]), 'fsdp', split_axis=0,...]
    dot_general x9 -> x14, matrix products: 60.2 us -> 79.5 us  [the longest x2 11.7 us: place_back(): jnp.einsum('ebrt,ebrd->btd', select, rows, preferred_element_type=f32)]
    scatter x1 -> x0, local copies, waits for them, and re-layouts: 13.3 us -> none  [fill_buffer(): jnp.zeros((EXPERTS * CAP, width), jnp.bfloat16).at[slot].set(values)]
    mul x5 -> x1, local copies, waits for them, and re-layouts: 8.66 us -> 0.08 us  [on_device(): weighted = (row_prob * hidden).astype(jnp.bfloat16)]
  transfers between devices with their start and end apart: 6 -> 0, of which waited for: 5 -> 0; matrix products, arithmetic and copies ran while one was open for 16% -> 0% of each run, Pallas kernels for 0% -> 0%
where the time goes in v1:
time: 330 us; the launch traced here: 325 us
  Pallas kernels  179 us (54%)
  matrix products  79.5 us (24%)
  blocking collectives  54.8 us (17%)
  other arithmetic  5.68 us (2%)
  local copies, waits for them, and re-layouts  5.67 us (2%)
    pallas_call x1, Pallas kernels, gather_pair(): pl.pallas_call(gather_kernel, out_shape=(full, full), in_specs=[pl.BlockS...  89.5 us
    pallas_call x1, Pallas kernels, scatter_pair(): pl.pallas_call(scatter_kernel, out_shape=(out, out), in_specs=[pl.BlockSp...  89.3 us
    psum x1, blocking collectives, on_device(): d_prob = lax.psum(d_prob.reshape(blocks, topk * tok_rows), ('fsdp', 'tok'))  39 us
    all_gather x1, blocking collectives, on_device(): routes = lax.all_gather(routes, 'fsdp', axis=0, tiled=False)  15.8 us
    dot_general x2, matrix products, place_back(): jnp.einsum('ebrt,ebrd->btd', select, rows, preferred_element_type=f32)  11.7 us
    dot_general x2, matrix products, pick(): jnp.einsum('ebrt,btd->ebrd', select, values, preferred_element_type=f32)  9.35 us
    dot_general x1, matrix products, on_device(): jnp.einsum('erd,ehd->erh', cotangent, w_down, preferred_element_type=f32)  8.03 us
    dot_general x1, matrix products, on_device(): jnp.einsum('erh,ehd->erd', d_upper, w_up, preferred_element_type=f32)  7.93 us

profile of v1, /device:TPU:11, one launch (start us, length us, event | category | flops | bytes accessed | tf_op | source)
XLA Modules:
  0.0 325.3 jit_solution(103600033014055898)
XLA Ops:
  0.7 0.7 convert_bitcast_fusion.2
  1.3 0.7 pad_maximum_fusion
  2.0 15.8 %all-gather = f32[128,128]{1,0:T(8,128)S(1)} all-gather(f32[8,128]{1,0:T(8,128)S(1)} %pad_maximum_fusion), channel_id=2, replica_groups=mesh['fsdp'=16,'tok'=2] {'fsdp'}, dimensions={0}, use_global_device_ids=true | all-gather | bytes 69632 | tf_op jit(solution)/shard_map/all_gather | solution.py:320
  17.9 0.1 compare_reduce_fusion
  18.0 0.1 convolution_select_fusion
  18.1 89.5 %shard_map.118 = (bf16[16,128,2048]{2,1,0:T(8,128)(2,1)}, bf16[16,128,2048]{2,1,0:T(8,128)(2,1)}) custom-call(bf16[128,1024]{1,0:T(8,128)(2,1)} %in0.1, bf16[128,1024]{1,0:T(8,128)(2,1)} %in1.1), custom_call_target="tpu_custom_call" | custom-call | tf_op jit(solution)/shard_map/pallas_call | solution.py:157
  107.6 4.7 %convert_bitcast_fusion.1 = bf16[2,16,32,2048]{3,2,0,1:T(8,128)(2,1)S(1)} fusion(bf16[16,128,2048]{2,1,0:T(8,128)(2,1)} %get-tuple-element.10, f32[2,16,128]{2,0,1:T(2,128)S(1)} %copy.49, f32[32]{0:T(128)S(1)} %iota_convert_fusion), kind=kOutput, calls=%fused_computation.10 | convolution fusion | flops 539099136 | bytes 12599424 | tf_op jit(solution)/shard_map/ebrt,btd->ebrd/dot_general | solution.py:341
  112.3 0.3 copy.53
  112.6 7.2 %fusion.36 = f32[2,512,704]{1,2,0:T(8,128)S(1)} fusion(bf16[2,512,2048]{2,1,0:T(8,128)(2,1)S(1)} %bitcast.64, bf16[2,704,2048]{2,1,0:T(8,128)(2,1)} %param.11), kind=kOutput, calls=%fused_computation.55 | convolution fusion | flops 2952790016 | bytes 12845056 | tf_op jit(solution)/shard_map/erd,ehd->erh/dot_general | solution.py:352
  119.9 4.8 %fusion.35 = f32[2,512,704]{1,2,0:T(8,128)} fusion(bf16[2,512,2048]{2,1,0:T(8,128)(2,1)S(1)} %bitcast.65, bf16[2,704,2048]{2,1,0:T(8,128)(2,1)S(1)} %bitcast.74), kind=kOutput, calls=%fused_computation.54 | convolution fusion | flops 2952790016 | bytes 12845056 | tf_op jit(solution)/shard_map/erd,ehd->erh/dot_general | solution.py:351
  124.6 4.7 %convert_bitcast_fusion = bf16[2,16,32,2048]{3,2,0,1:T(8,128)(2,1)S(1)} fusion(bf16[16,128,2048]{2,1,0:T(8,128)(2,1)} %get-tuple-element.11, f32[2,16,128]{2,0,1:T(2,128)S(1)} %copy.49, f32[32]{0:T(128)S(1)} %iota_convert_fusion), kind=kOutput, calls=%fused_computation.9 | convolution fusion | flops 539099136 | bytes 12599424 | tf_op jit(solution)/shard_map/ebrt,btd->ebrd/dot_general | solution.py:341
  129.3 0.3 copy.55
  129.6 2.8 copy-done.4
  132.4 8.0 %multiply_reduce_fusion = (f32[2,512]{1,0:T(2,128)S(1)}, f32[2,512,704]{1,2,0:T(8,128)}) fusion(f32[2,512,704]{1,2,0:T(8,128)S(1)} %fusion.36, f32[2,512,704]{1,2,0:T(8,128)S(1)} %copy-done.4, bf16[2,512,2048]{2,1,0:T(8,128)(2,1)S(1)} %bitcast.68, bf16[2,704,2048]{2,1,0:T(8,128)(2,1)} %param.12), kind=kOutput, calls=%fused_computation.12 | convolution fusion | flops 2957835264 | bytes 18616320 | tf_op jit(solution)/shard_map/erd,ehd->erh/dot_general | solution.py:353
  140.5 0.2 fusion.16
  140.8 0.1 fusion.26
  140.9 39.0 %psum.7 = f32[16,512]{1,0:T(8,128)S(1)} all-reduce(f32[16,512]{1,0:T(8,128)S(1)} %copy_bitcast_fusion), channel_id=1, replica_groups=mesh['fsdp'=16,'tok'=2] {'fsdp','tok'}, use_global_device_ids=true, to_apply=%region_6.7 | all-reduce | flops 8192 | bytes 65536 | tf_op jit(solution)/shard_map/psum | solution.py:378
  179.8 0.6 constant_dynamic-slice_fusion
  180.4 0.3 fusion.15
  180.8 0.1 mul.44
  180.8 3.6 %multiply_convert_fusion = (bf16[2,512,704]{1,2,0:T(8,128)(2,1)S(1)}, bf16[2,512,704]{1,2,0:T(8,128)(2,1)S(1)}, bf16[2,512,704]{1,2,0:T(8,128)(2,1)S(1)}) fusion(f32[2,512,704]{1,2,0:T(8,128)} %get-tuple-element.22, f32[2,512]{1,0:T(2,128)S(1)} %mul.44, f32[2,512,704]{1,2,0:T(8,128)} %fusion.35, f32[2,512,704]{1,2,0:T(8,128)S(1)} %fusion.36), kind=kLoop, calls=%fused_computation.13 | loop fusion | flops 12255232 | bytes 12980224 | tf_op jit(solution)/shard_map/convert_element_type | solution.py:360
  184.5 6.4 %convolution_convert_fusion = bf16[2,512,2048]{2,1,0:T(8,128)(2,1)S(1)} fusion(bf16[2,512,704]{1,2,0:T(8,128)(2,1)S(1)} %get-tuple-element.18, bf16[2,704,2048]{2,1,0:T(8,128)(2,1)} %param.12), kind=kOutput, calls=%fused_computation.11 | convolution fusion | flops 2954887168 | bytes 11403264 | tf_op jit(solution)/shard_map/erh,ehd->erd/dot_general | solution.py:363
  190.9 5.9 %bitcast_convert_fusion.1.in0 = bf16[16,128,2048]{2,1,0:T(8,128)(2,1)} fusion(bf16[2,16,32,2048]{3,2,1,0:T(8,128)(2,1)S(1)} %bitcast.63, f32[2,16,128]{2,0,1:T(2,128)S(1)} %copy.49, f32[32]{0:T(128)S(1)} %iota_convert_fusion), kind=kOutput, calls=%fused_computation.1 | convolution fusion | flops 541196288 | bytes 12599424 | tf_op jit(solution)/shard_map/ebrt,ebrd->btd/dot_general | solution.py:346
  196.7 6.1 %fusion.40 = f32[2,704,2048]{2,1,0:T(8,128)} fusion(bf16[2,512,704]{1,2,0:T(8,128)(2,1)S(1)} %get-tuple-element.18, bf16[2,512,2048]{2,1,0:T(8,128)(2,1)S(1)} %bitcast.69), kind=kOutput, calls=%fused_computation.59 | convolution fusion | flops 2952790016 | bytes 17170432 | tf_op jit(solution)/shard_map/erh,erd->ehd/dot_general | solution.py:372
  202.8 5.7 %fusion.37 = f32[2,512,2048]{2,1,0:T(8,128)} fusion(bf16[2,512,704]{1,2,0:T(8,128)(2,1)S(1)} %get-tuple-element.17, bf16[2,704,2048]{2,1,0:T(8,128)(2,1)S(1)} %bitcast.76), kind=kOutput, calls=%fused_computation.56 | convolution fusion | flops 2952790016 | bytes 15597568 | tf_op jit(solution)/shard_map/erh,ehd->erd/dot_general | solution.py:364
  208.5 7.9 %add_convert_fusion = bf16[2,512,2048]{2,1,0:T(8,128)(2,1)S(1)} fusion(f32[2,512,2048]{2,1,0:T(8,128)} %fusion.37, bf16[2,512,704]{1,2,0:T(8,128)(2,1)S(1)} %get-tuple-element.16, bf16[2,704,2048]{2,1,0:T(8,128)(2,1)} %param.11), kind=kOutput, calls=%fused_computation.6 | convolution fusion | flops 2956984320 | bytes 19791872 | tf_op jit(solution)/shard_map/erh,ehd->erd/dot_general | solution.py:365
  216.5 5.9 %bitcast_convert_fusion.in1 = bf16[16,128,2048]{2,1,0:T(8,128)(2,1)} fusion(bf16[2,16,32,2048]{3,2,1,0:T(8,128)(2,1)S(1)} %bitcast.62, f32[2,16,128]{2,0,1:T(2,128)S(1)} %copy.49, f32[32]{0:T(128)S(1)} %iota_convert_fusion), kind=kOutput, calls=%fused_computation | convolution fusion | flops 541196288 | bytes 12599424 | tf_op jit(solution)/shard_map/ebrt,ebrd->btd/dot_general | solution.py:346
  222.3 89.3 %shard_map.119 = (bf16[128,1024]{1,0:T(8,128)(2,1)S(1)}, bf16[128,1024]{1,0:T(8,128)(2,1)S(1)}) custom-call(bf16[16,128,2048]{2,1,0:T(8,128)(2,1)} %bitcast_convert_fusion.1.in0, bf16[16,128,2048]{2,1,0:T(8,128)(2,1)} %bitcast_convert_fusion.in1), custom_call_target="tpu_custom_call" | custom-call | tf_op jit(solution)/shard_map/pallas_call | solution.py:278
  311.7 6.1 %fusion.39 = f32[2,704,2048]{2,1,0:T(8,128)} fusion(bf16[2,512,704]{1,2,0:T(8,128)(2,1)S(1)} %get-tuple-element.16, bf16[2,512,2048]{2,1,0:T(8,128)(2,1)S(1)} %bitcast.66), kind=kOutput, calls=%fused_computation.58 | convolution fusion | flops 2952790016 | bytes 17170432 | tf_op jit(solution)/shard_map/erh,erd->ehd/dot_general | solution.py:374
  317.8 6.1 %fusion.38 = f32[2,704,2048]{2,1,0:T(8,128)} fusion(bf16[2,512,704]{1,2,0:T(8,128)(2,1)S(1)} %get-tuple-element.17, bf16[2,512,2048]{2,1,0:T(8,128)(2,1)S(1)} %bitcast.67), kind=kOutput, calls=%fused_computation.57 | convolution fusion | flops 2952790016 | bytes 17170432 | tf_op jit(solution)/shard_map/erh,erd->ehd/dot_general | solution.py:373
  323.9 0.7 copy.72
  324.6 0.7 copy.73
  (31 shorter events, 0.2 us)
Async XLA Ops:
  112.3 7.6 %slice-start = ((s8[5767168]{0:T(1024)(128)(4,1)}), s8[4194304]{0:T(1024)(128)(4,1)S(1)}, s32[]{:S(2)}) async-start(s8[5767168]{0:T(1024)(128)(4,1)} %bitcast.73), calls=%async_computation | async-start | bytes 8388608
  112.6 7.2 %copy-start = (bf16[2,16,32,2048]{3,2,1,0:T(8,128)(2,1)}, bf16[2,16,32,2048]{3,2,1,0:T(8,128)(2,1)S(1)}, u32[]{:S(2)}) copy-start(bf16[2,16,32,2048]{3,2,1,0:T(8,128)(2,1)S(1)} %copy.53) | copy-start | bytes 12582916
  112.6 7.2 %slice-start.1 = ((s8[5767168]{0:T(1024)(128)(4,1)}), s8[1572864]{0:T(1024)(128)(4,1)S(1)}, s32[]{:S(2)}) async-start(s8[5767168]{0:T(1024)(128)(4,1)} %bitcast.73), calls=%async_computation.1 | async-start | bytes 3145728
  129.3 3.1 copy-start.4
  129.6 10.8 %copy-start.2 = (bf16[2,16,32,2048]{3,2,1,0:T(8,128)(2,1)}, bf16[2,16,32,2048]{3,2,1,0:T(8,128)(2,1)S(1)}, u32[]{:S(2)}) copy-start(bf16[2,16,32,2048]{3,2,1,0:T(8,128)(2,1)S(1)} %copy.55) | copy-start | bytes 12582916
  190.8 5.9 %copy-start.3 = (bf16[2,16,32,2048]{3,2,1,0:T(8,128)(2,1)S(1)}, bf16[2,16,32,2048]{3,2,1,0:T(8,128)(2,1)}, u32[]{:S(2)}) copy-start(bf16[2,16,32,2048]{3,2,1,0:T(8,128)(2,1)} %copy-done.2) | copy-start | bytes 12582916
  190.8 12.0 %slice-start.2 = ((s8[5767168]{0:T(1024)(128)(4,1)}), s8[4194304]{0:T(1024)(128)(4,1)S(1)}, s32[]{:S(2)}) async-start(s8[5767168]{0:T(1024)(128)(4,1)} %bitcast.75), calls=%async_computation.2 | async-start | bytes 8388608
  196.7 6.1 %slice-start.3 = ((s8[5767168]{0:T(1024)(128)(4,1)}), s8[1572864]{0:T(1024)(128)(4,1)S(1)}, s32[]{:S(2)}) async-start(s8[5767168]{0:T(1024)(128)(4,1)} %bitcast.75), calls=%async_computation.3 | async-start | bytes 3145728
  222.3 89.3 %copy-start.1 = (bf16[2,16,32,2048]{3,2,1,0:T(8,128)(2,1)S(1)}, bf16[2,16,32,2048]{3,2,1,0:T(8,128)(2,1)}, u32[]{:S(2)}) copy-start(bf16[2,16,32,2048]{3,2,1,0:T(8,128)(2,1)} %copy-done) | copy-start | bytes 12582916

commit v2 on v1

--- a/solution.py
+++ b/solution.py
@@ -375,8 +375,14 @@
 
     d_prob = jnp.sum(jnp.where(filled, d_rows[:, :, :, None], 0.0), axis=2)
     d_prob = jnp.sum(jnp.where(chosen, d_prob[:, :, None, :], 0.0), axis=0)
-    d_prob = lax.psum(d_prob.reshape(blocks, topk * tok_rows), ("fsdp", "tok"))
-    d_prob = lax.dynamic_index_in_dim(d_prob, me, 0, keepdims=False)
+    d_prob = d_prob.reshape(blocks, topk * tok_rows)
+    d_prob = lax.all_to_all(d_prob, "fsdp", split_axis=0, concat_axis=0, tiled=True)
+    d_prob = jnp.sum(d_prob, axis=0)
+    size = lax.axis_size("tok")
+    mine_only = d_prob
+    for turn in range(1, size):
+        pairs = [(i, (i + turn) % size) for i in range(size)]
+        d_prob = d_prob + lax.ppermute(mine_only, "tok", pairs)
     d_gate_probs = d_prob.reshape(topk, tok_rows).T
     return (layer_out, d_tokens, d_gate_probs, d_w_gate, d_w_up, d_w_down)
 

time: 330 us -> 297 us (0.900)
  blocking collectives: 54.8 us -> 15.8 us
  starting transfers between devices: 0 us -> 6.32 us
    psum x1 -> x0, blocking collectives: 39 us -> none  [on_device(): d_prob = lax.psum(d_prob.reshape(blocks, topk * tok_rows), ('fsdp', 'tok'))]
    all_to_all x0 -> x1, starting transfers between devices: none -> 5.98 us  [on_device(): lax.all_to_all(d_prob, 'fsdp', split_axis=0, concat_axis=0, tiled=True)]
  transfers between devices with their start and end apart: 0 -> 2, of which waited for: 0 -> 0; matrix products, arithmetic and copies ran while one was open for 0% -> 18% of each run, Pallas kernels for 0% -> 31%
where the time goes in v2:
time: 297 us; the launch traced here: 292 us
  Pallas kernels  180 us (61%)
  matrix products  76.8 us (26%)
  blocking collectives  15.8 us (5%)
  other arithmetic  6.45 us (2%)
  starting transfers between devices  6.32 us (2%)
  local copies, waits for them, and re-layouts  5.72 us (2%)
    pallas_call x1, Pallas kernels, scatter_pair(): pl.pallas_call(scatter_kernel, out_shape=(out, out), in_specs=[pl.BlockSp...  90.4 us
    pallas_call x1, Pallas kernels, gather_pair(): pl.pallas_call(gather_kernel, out_shape=(full, full), in_specs=[pl.BlockS...  89.5 us
    all_gather x1, blocking collectives, on_device(): routes = lax.all_gather(routes, 'fsdp', axis=0, tiled=False)  15.8 us
    dot_general x2, matrix products, place_back(): jnp.einsum('ebrt,ebrd->btd', select, rows, preferred_element_type=f32)  13.5 us
    dot_general x2, matrix products, pick(): jnp.einsum('ebrt,btd->ebrd', select, values, preferred_element_type=f32)  9.36 us
    dot_general x1, matrix products, on_device(): jnp.einsum('erd,ehd->erh', cotangent, w_down, preferred_element_type=f32)  8.03 us
    dot_general x1, matrix products, on_device(): upper = jnp.einsum('erd,ehd->erh', inputs, w_up, preferred_element_type=f32)  7.19 us
    dot_general x1, matrix products, on_device(): jnp.einsum('erh,ehd->erd', weighted, w_down, preferred_element_type=f32)  6.52 us
  transfers between devices with their start and end apart: 2, of which 0 were waited for; matrix products, arithmetic and copies ran while one was open for 18% of the time, Pallas kernels for 31%

profile of v2, /device:TPU:11, one launch (start us, length us, event | category | flops | bytes accessed | tf_op | source)
XLA Modules:
  0.0 291.9 jit_solution(18321603893037328756)
XLA Ops:
  0.7 0.7 convert_bitcast_fusion.2
  1.3 0.7 pad_maximum_fusion
  2.0 15.8 %all-gather = f32[128,128]{1,0:T(8,128)S(1)} all-gather(f32[8,128]{1,0:T(8,128)S(1)} %pad_maximum_fusion), channel_id=2, replica_groups=mesh['fsdp'=16,'tok'=2] {'fsdp'}, dimensions={0}, use_global_device_ids=true | all-gather | bytes 69632 | tf_op jit(solution)/shard_map/all_gather | solution.py:320
  18.0 0.1 convolution_select_fusion
  18.1 89.5 %shard_map.118 = (bf16[16,128,2048]{2,1,0:T(8,128)(2,1)}, bf16[16,128,2048]{2,1,0:T(8,128)(2,1)}) custom-call(bf16[128,1024]{1,0:T(8,128)(2,1)} %in0.1, bf16[128,1024]{1,0:T(8,128)(2,1)} %in1.1), custom_call_target="tpu_custom_call" | custom-call | tf_op jit(solution)/shard_map/pallas_call | solution.py:157
  107.6 4.7 %convert_bitcast_fusion.1 = bf16[2,16,32,2048]{3,2,0,1:T(8,128)(2,1)S(1)} fusion(bf16[16,128,2048]{2,1,0:T(8,128)(2,1)} %get-tuple-element.10, f32[2,16,128]{2,0,1:T(2,128)S(1)} %copy.49, f32[32]{0:T(128)S(1)} %iota_convert_fusion), kind=kOutput, calls=%fused_computation.10 | convolution fusion | flops 539099136 | bytes 12599424 | tf_op jit(solution)/shard_map/ebrt,btd->ebrd/dot_general | solution.py:341
  112.3 0.3 copy.53
  112.6 7.2 %fusion.36 = f32[2,512,704]{1,2,0:T(8,128)S(1)} fusion(bf16[2,512,2048]{2,1,0:T(8,128)(2,1)S(1)} %bitcast.61, bf16[2,704,2048]{2,1,0:T(8,128)(2,1)} %param.11), kind=kOutput, calls=%fused_computation.54 | convolution fusion | flops 2952790016 | bytes 12845056 | tf_op jit(solution)/shard_map/erd,ehd->erh/dot_general | solution.py:352
  119.9 4.7 %fusion.35 = f32[2,512,704]{1,2,0:T(8,128)} fusion(bf16[2,512,2048]{2,1,0:T(8,128)(2,1)S(1)} %bitcast.62, bf16[2,704,2048]{2,1,0:T(8,128)(2,1)S(1)} %bitcast.70), kind=kOutput, calls=%fused_computation.53 | convolution fusion | flops 2952790016 | bytes 12845056 | tf_op jit(solution)/shard_map/erd,ehd->erh/dot_general | solution.py:351
  124.6 4.7 %convert_bitcast_fusion = bf16[2,16,32,2048]{3,2,0,1:T(8,128)(2,1)S(1)} fusion(bf16[16,128,2048]{2,1,0:T(8,128)(2,1)} %get-tuple-element.11, f32[2,16,128]{2,0,1:T(2,128)S(1)} %copy.49, f32[32]{0:T(128)S(1)} %iota_convert_fusion), kind=kOutput, calls=%fused_computation.9 | convolution fusion | flops 539099136 | bytes 12599424 | tf_op jit(solution)/shard_map/ebrt,btd->ebrd/dot_general | solution.py:341
  129.3 0.3 copy.55
  129.6 2.8 copy-done.4
  132.4 8.0 %multiply_reduce_fusion = (f32[2,512]{1,0:T(2,128)S(1)}, f32[2,512,704]{1,2,0:T(8,128)}) fusion(f32[2,512,704]{1,2,0:T(8,128)S(1)} %fusion.36, f32[2,512,704]{1,2,0:T(8,128)S(1)} %copy-done.4, bf16[2,512,2048]{2,1,0:T(8,128)(2,1)S(1)} %bitcast.65, bf16[2,704,2048]{2,1,0:T(8,128)(2,1)} %param.12), kind=kOutput, calls=%fused_computation.12 | convolution fusion | flops 2957835264 | bytes 18616320 | tf_op jit(solution)/shard_map/erd,ehd->erh/dot_general | solution.py:353
  140.5 0.2 fusion.16
  140.8 0.1 fusion.26
  140.9 0.6 copy.59
  141.5 6.0 %all-to-all-start = ((f32[16,1,512]{2,1,0:T(1,128)}), f32[16,1,512]{2,1,0:T(1,128)S(1)}, u32[]{:S(2)}, u32[]{:S(2)}) async-start(f32[16,1,512]{2,1,0:T(1,128)} %bitcast.18), calls=%async_computation | async-start | bytes 65536 | tf_op jit(solution)/shard_map/all_to_all | solution.py:379
  147.5 0.3 fusion.15
  147.9 3.7 %multiply_convert_fusion = (bf16[2,512,704]{1,2,0:T(8,128)(2,1)S(1)}, bf16[2,512,704]{1,2,0:T(8,128)(2,1)S(1)}, bf16[2,512,704]{1,2,0:T(8,128)(2,1)S(1)}) fusion(f32[2,512,704]{1,2,0:T(8,128)} %get-tuple-element.22, f32[2,512]{1,0:T(2,128)S(1)} %mul.44, f32[2,512,704]{1,2,0:T(8,128)} %fusion.35, f32[2,512,704]{1,2,0:T(8,128)S(1)} %fusion.36), kind=kLoop, calls=%fused_computation.13 | loop fusion | flops 12255232 | bytes 12980224 | tf_op jit(solution)/shard_map/convert_element_type | solution.py:360
  151.7 6.5 %convolution_convert_fusion = bf16[2,512,2048]{2,1,0:T(8,128)(2,1)S(1)} fusion(bf16[2,512,704]{1,2,0:T(8,128)(2,1)S(1)} %get-tuple-element.18, bf16[2,704,2048]{2,1,0:T(8,128)(2,1)} %param.12), kind=kOutput, calls=%fused_computation.11 | convolution fusion | flops 2954887168 | bytes 11403264 | tf_op jit(solution)/shard_map/erh,ehd->erd/dot_general | solution.py:363
  158.2 6.1 %fusion.40 = f32[2,704,2048]{2,1,0:T(8,128)} fusion(bf16[2,512,704]{1,2,0:T(8,128)(2,1)S(1)} %get-tuple-element.18, bf16[2,512,2048]{2,1,0:T(8,128)(2,1)S(1)} %bitcast.66), kind=kOutput, calls=%fused_computation.58 | convolution fusion | flops 2952790016 | bytes 17170432 | tf_op jit(solution)/shard_map/erh,erd->ehd/dot_general | solution.py:372
  164.3 3.6 %fusion.37 = f32[2,512,2048]{2,1,0:T(8,128)S(1)} fusion(bf16[2,512,704]{1,2,0:T(8,128)(2,1)S(1)} %get-tuple-element.17, bf16[2,704,2048]{2,1,0:T(8,128)(2,1)S(1)} %bitcast.72), kind=kOutput, calls=%fused_computation.55 | convolution fusion | flops 2952790016 | bytes 15597568 | tf_op jit(solution)/shard_map/erh,ehd->erd/dot_general | solution.py:364
  168.0 6.1 %fusion.38 = f32[2,704,2048]{2,1,0:T(8,128)} fusion(bf16[2,512,704]{1,2,0:T(8,128)(2,1)S(1)} %get-tuple-element.17, bf16[2,512,2048]{2,1,0:T(8,128)(2,1)S(1)} %bitcast.63), kind=kOutput, calls=%fused_computation.56 | convolution fusion | flops 2952790016 | bytes 17170432 | tf_op jit(solution)/shard_map/erh,erd->ehd/dot_general | solution.py:373
  174.1 6.1 %fusion.39 = f32[2,704,2048]{2,1,0:T(8,128)} fusion(bf16[2,512,704]{1,2,0:T(8,128)(2,1)S(1)} %get-tuple-element.16, bf16[2,512,2048]{2,1,0:T(8,128)(2,1)S(1)} %bitcast.64), kind=kOutput, calls=%fused_computation.57 | convolution fusion | flops 2952790016 | bytes 17170432 | tf_op jit(solution)/shard_map/erh,erd->ehd/dot_general | solution.py:374
  180.2 5.3 %add_convert_fusion = bf16[2,512,2048]{2,1,0:T(8,128)(2,1)} fusion(f32[2,512,2048]{2,1,0:T(8,128)S(1)} %fusion.37, bf16[2,512,704]{1,2,0:T(8,128)(2,1)S(1)} %get-tuple-element.16, bf16[2,704,2048]{2,1,0:T(8,128)(2,1)S(1)} %bitcast.74), kind=kOutput, calls=%fused_computation.6 | convolution fusion | flops 2956984320 | bytes 19791872 | tf_op jit(solution)/shard_map/erh,ehd->erd/dot_general | solution.py:365
  185.6 5.7 %bitcast_convert_fusion.1.in0 = bf16[16,128,2048]{2,1,0:T(8,128)(2,1)} fusion(bf16[2,16,32,2048]{3,2,1,0:T(8,128)(2,1)S(1)} %bitcast.60, f32[2,16,128]{2,0,1:T(2,128)S(1)} %copy.49, f32[32]{0:T(128)S(1)} %iota_convert_fusion), kind=kOutput, calls=%fused_computation.1 | convolution fusion | flops 541196288 | bytes 12599424 | tf_op jit(solution)/shard_map/ebrt,ebrd->btd/dot_general | solution.py:346
  191.3 0.3 collective-permute-start
  191.6 7.9 %bitcast_convert_fusion.in1 = bf16[16,128,2048]{2,1,0:T(8,128)(2,1)} fusion(bf16[2,16,32,2048]{3,2,1,0:T(8,128)(2,1)} %bitcast.59, f32[2,16,128]{2,0,1:T(2,128)S(1)} %copy.49, f32[32]{0:T(128)S(1)} %iota_convert_fusion), kind=kOutput, calls=%fused_computation | convolution fusion | flops 541196288 | bytes 12599424 | tf_op jit(solution)/shard_map/ebrt,ebrd->btd/dot_general | solution.py:346
  199.5 90.4 %shard_map.119 = (bf16[128,1024]{1,0:T(8,128)(2,1)S(1)}, bf16[128,1024]{1,0:T(8,128)(2,1)S(1)}) custom-call(bf16[16,128,2048]{2,1,0:T(8,128)(2,1)} %bitcast_convert_fusion.1.in0, bf16[16,128,2048]{2,1,0:T(8,128)(2,1)} %bitcast_convert_fusion.in1), custom_call_target="tpu_custom_call" | custom-call | tf_op jit(solution)/shard_map/pallas_call | solution.py:278
  289.9 0.6 add_bitcast_fusion
  290.5 0.7 copy.71
  291.2 0.7 copy.72
  (40 shorter events, 0.4 us)
Async XLA Ops:
  112.3 7.6 %slice-start = ((s8[5767168]{0:T(1024)(128)(4,1)}), s8[4194304]{0:T(1024)(128)(4,1)S(1)}, s32[]{:S(2)}) async-start(s8[5767168]{0:T(1024)(128)(4,1)} %bitcast.69), calls=%async_computation.1 | async-start | bytes 8388608
  112.6 7.2 %copy-start = (bf16[2,16,32,2048]{3,2,1,0:T(8,128)(2,1)}, bf16[2,16,32,2048]{3,2,1,0:T(8,128)(2,1)S(1)}, u32[]{:S(2)}) copy-start(bf16[2,16,32,2048]{3,2,1,0:T(8,128)(2,1)S(1)} %copy.53) | copy-start | bytes 12582916
  112.6 7.2 %slice-start.1 = ((s8[5767168]{0:T(1024)(128)(4,1)}), s8[1572864]{0:T(1024)(128)(4,1)S(1)}, s32[]{:S(2)}) async-start(s8[5767168]{0:T(1024)(128)(4,1)} %bitcast.69), calls=%async_computation.2 | async-start | bytes 3145728
  129.3 3.1 %copy-start.4 = (f32[2,512,704]{1,2,0:T(8,128)S(1)}, f32[2,512,704]{1,2,0:T(8,128)}, u32[]{:S(2)}) copy-start(f32[2,512,704]{1,2,0:T(8,128)} %fusion.35) | copy-start | bytes 8650756
  129.6 10.8 %copy-start.2 = (bf16[2,16,32,2048]{3,2,1,0:T(8,128)(2,1)}, bf16[2,16,32,2048]{3,2,1,0:T(8,128)(2,1)S(1)}, u32[]{:S(2)}) copy-start(bf16[2,16,32,2048]{3,2,1,0:T(8,128)(2,1)S(1)} %copy.55) | copy-start | bytes 12582916
  141.5 49.8 %all-to-all-start = ((f32[16,1,512]{2,1,0:T(1,128)}), f32[16,1,512]{2,1,0:T(1,128)S(1)}, u32[]{:S(2)}, u32[]{:S(2)}) async-start(f32[16,1,512]{2,1,0:T(1,128)} %bitcast.18), calls=%async_computation | async-start | bytes 65536 | tf_op jit(solution)/shard_map/all_to_all | solution.py:379
  147.9 16.4 %slice-start.2 = ((s8[5767168]{0:T(1024)(128)(4,1)}), s8[4194304]{0:T(1024)(128)(4,1)S(1)}, s32[]{:S(2)}) async-start(s8[5767168]{0:T(1024)(128)(4,1)} %bitcast.71), calls=%async_computation.3 | async-start | bytes 8388608
  151.7 6.6 %copy-start.3 = (bf16[2,16,32,2048]{3,2,1,0:T(8,128)(2,1)S(1)}, bf16[2,16,32,2048]{3,2,1,0:T(8,128)(2,1)}, u32[]{:S(2)}) copy-start(bf16[2,16,32,2048]{3,2,1,0:T(8,128)(2,1)} %copy-done.2) | copy-start | bytes 12582916
  151.7 12.7 %slice-start.3 = ((s8[5767168]{0:T(1024)(128)(4,1)}), s8[1572864]{0:T(1024)(128)(4,1)S(1)}, s32[]{:S(2)}) async-start(s8[5767168]{0:T(1024)(128)(4,1)} %bitcast.71), calls=%async_computation.4 | async-start | bytes 3145728
  164.3 3.6 %copy-start.1 = (bf16[2,16,32,2048]{3,2,1,0:T(8,128)(2,1)S(1)}, bf16[2,16,32,2048]{3,2,1,0:T(8,128)(2,1)}, u32[]{:S(2)}) copy-start(bf16[2,16,32,2048]{3,2,1,0:T(8,128)(2,1)} %copy-done) | copy-start | bytes 12582916
  168.0 12.2 %slice-start.4 = ((s8[5767168]{0:T(1024)(128)(4,1)}), s8[4194304]{0:T(1024)(128)(4,1)S(1)}, s32[]{:S(2)}) async-start(s8[5767168]{0:T(1024)(128)(4,1)} %bitcast.73), calls=%async_computation.5 | async-start | bytes 8388608
  174.1 6.1 %slice-start.5 = ((s8[5767168]{0:T(1024)(128)(4,1)}), s8[1572864]{0:T(1024)(128)(4,1)S(1)}, s32[]{:S(2)}) async-start(s8[5767168]{0:T(1024)(128)(4,1)} %bitcast.73), calls=%async_computation.6 | async-start | bytes 3145728
  191.3 98.6 %collective-permute-start = (f32[512]{0:T(512)S(1)}, f32[512]{0:T(512)S(1)}, u32[]{:S(2)}, u32[]{:S(2)}) collective-permute-start(f32[512]{0:T(512)S(1)} %reduce_sum.59), channel_id=1, source_target_pairs={{0,1},{1,0},{2,3},{3,2},{4,5},{5,4},{6,7},{7,6},{8,9},{9,8},{10,11... | collective-permute-start | bytes 6152 | tf_op jit(solution)/shard_map/ppermute | solution.py:385
